TPU v7x, 32 devices: a whole 2x2x4 slice. The times are simulated.
32 devices in a mesh: farm: 2 (over y), clus: 4 (over x, core), lag: 4 (over z).
Axes of the slice: x: 2, y: 2, z: 4, core: 2. Of those that a mesh axis runs over, the one named last changes fastest.
Arguments:
- history: bfloat16 [8, 256, 2048], P(None, ('farm', 'lag'), 'clus'), parts along dimension 1, may hold values from -6 to 6
- kernel: bfloat16 [8, 2048, 2048], P('lag', 'clus'), may hold values from -0.046875 to 0.046875
- moments: bfloat16 [8, 8, 256], P(None, ('farm', 'clus')), parts along dimension 1, may hold values from -6 to 6
- coupling: bfloat16 [4, 3, 8, 256, 256], P('clus', None, 'lag'), may hold values from -0.078125 to 0.078125
- evaluation: float32 [256, 2048], replicated, may hold values from -0.375 to 0.375
- offsets: int32 [8], replicated, may hold values from 0 to 7, as said below
- pair_sources: int32 [4, 3], replicated, may hold values from 0 to 3, as said below
- body_cluster: int32 [128], replicated, may hold values from 0 to 3, as said below
Outputs:
- total: bfloat16 [256, 2048], P(('farm', 'lag'), 'clus'), parts along dimension 0
There are 2 independent parts, one for each index of `farm`. A program takes and returns all parts, laid end to end along the dimension named above; an argument that names none is the same for every part. Nothing has to cross between parts.
Inputs may be any that keep to these rules, and one draw needn't show every extreme that they name: offsets lists every cycle slot exactly once. `pair_sources`: row d lists every cluster other than d exactly once. `body_cluster`: every cluster holds exactly 32 bodies.
All inputs are finite; a program needn't handle non-finite values.
Results may differ from a plain program's by a relative error of at most 0.0015.
Values may be sent and summed in bfloat16 or wider, within the bound.
A program may use at most 64 MiB of HBM per device.

v0:
```python
import jax
import jax.numpy as jnp
from jax import lax
from jax.sharding import PartitionSpec as P


def shards(history, kernel, moments, coupling, evaluation, offsets, pair_sources, body_cluster):
    lag_index = lax.axis_index("lag")
    clus_index = lax.axis_index("clus")
    clus_count = lax.axis_size("clus")
    lags_here = kernel.shape[0]
    panel_block = history.shape[2]
    body_block = history.shape[1]
    picked = jnp.take(history, offsets, axis=0)
    arrived = lax.all_to_all(picked, "lag", split_axis=0, concat_axis=1, tiled=True)
    partial_value = jnp.einsum("lbp,lpq->bq", arrived, kernel, preferred_element_type=jnp.float32)
    my_lags = lag_index * lags_here + jnp.arange(lags_here)
    my_slots = jnp.take(offsets, my_lags, axis=0)
    wanted = jnp.take(moments, my_slots, axis=0)
    source_row = lax.dynamic_index_in_dim(pair_sources, clus_index, 0, keepdims=False)
    piece = lax.all_gather(wanted, "clus", axis=1, tiled=True)
    count = piece.shape[1]
    hits = (source_row[:, None] == jnp.arange(count)[None, :]).astype(jnp.float32)
    gathered = jnp.einsum("kn,lnm->klm", hits, piece.astype(jnp.float32))
    selected = gathered.astype(jnp.bfloat16)
    local_part = jnp.einsum(
        "klmn,kln->m", coupling[0], selected, preferred_element_type=jnp.float32
    )
    owned_rows = lax.psum_scatter(partial_value, "lag", scatter_dimension=0, tiled=True)
    owned = lax.psum_scatter(owned_rows, "clus", scatter_dimension=1, tiled=True)
    cluster_ids = jnp.arange(clus_count)
    placed = (cluster_ids == clus_index).astype(jnp.float32)[:, None] * local_part[None, :]
    expansion_all = lax.psum(placed, ("clus", "lag"))
    eval_block = lax.dynamic_slice_in_dim(evaluation, clus_index * panel_block, panel_block, 1)
    far_block = jnp.dot(expansion_all, eval_block, precision=lax.Precision.HIGHEST)
    my_clusters = lax.dynamic_slice_in_dim(body_cluster, lag_index * body_block, body_block, 0)
    chooser = (my_clusters[:, None] == cluster_ids[None, :]).astype(jnp.float32)
    owned = owned + jnp.dot(chooser, far_block, precision=lax.Precision.HIGHEST)
    return owned.astype(jnp.bfloat16)


def solution(mesh):
    in_specs = (
        P(None, ("farm", "lag"), "clus"),
        P("lag", "clus", None),
        P(None, ("farm", "clus"), None),
        P("clus", None, "lag", None, None),
        P(),
        P(),
        P(),
        P(),
    )
    out_specs = P(("farm", "lag"), "clus")
    return jax.shard_map(shards, mesh=mesh, in_specs=in_specs, out_specs=out_specs, check_vma=False)
```

profile of v0, /device:TPU:0, one launch (start us, length us, event | category | flops | bytes accessed | tf_op | source)
XLA Modules:
  0.0 95.0 jit_solution(5362513539577097453)
XLA Ops:
  6.5 0.0 copy-start
  6.5 0.0 reduce-scatter.3.cloned.1.call-start
  6.5 0.8 compare_select_fusion.4
  7.3 0.7 compare_and_fusion.1
  8.0 1.5 %gather_fusion = bf16[8,32,512]{2,1,0:T(8,128)(2,1)S(1)} fusion(bf16[8,32,512]{2,1,0:T(8,128)(2,1)} %param.8, s32[1024]{0:T(1024)S(1)} %pad_clamp_fusion.2), kind=kCustom, calls=%fused_computation | custom fusion | bytes 524320 | tf_op jit(solution)/shard_map/jit(_take)/gather | solution.py:14
  9.5 0.0 copy-start.1
  9.6 0.1 broadcast_select_fusion
  9.6 0.0 copy-start.3
  9.7 0.0 copy-start.4
  9.7 0.0 copy-start.2
  9.7 15.1 %all_to_all.18 = bf16[8,32,512]{2,1,0:T(8,128)(2,1)S(1)} all-to-all(bf16[8,32,512]{2,1,0:T(8,128)(2,1)S(1)} %broadcast_select_fusion), channel_id=1, replica_groups=mesh['farm'=2,'clus'=4,'lag'=4] {'lag'}, dimensions={0} | all-to-all | bytes 524288 | tf_op jit(solution)/shard_map/all_to_all | solution.py:15
  24.8 3.9 %convolution_bitcast_fusion = f32[128,2048]{1,0:T(8,128)} fusion(bf16[2,128,512]{2,1,0:T(8,128)(2,1)S(1)} %bitcast.35, bf16[2,512,2048]{2,1,0:T(8,128)(2,1)} %param.9), kind=kOutput, calls=%fused_computation.3 | convolution fusion | flops 536870912 | bytes 5505024 | tf_op jit(solution)/shard_map/lbp,lpq->bq/dot_general | solution.py:16
  28.8 0.0 reduce-scatter.3.cloned.1.call-update
  28.8 0.0 reduce-scatter.5.cloned.1.call-start
  28.9 0.0 copy-done.1
  28.9 0.6 gather_fusion.1
  29.5 0.0 copy-done.3
  29.6 0.6 gather_fusion.2
  30.1 0.0 copy-done.4
  30.1 0.1 dynamic_slice.10
  30.2 0.1 broadcast_select_fusion.1
  30.3 5.1 %all_gather.3 = bf16[2,4,256]{2,0,1:T(2,128)(2,1)S(1)} all-gather(bf16[2,1,256]{2,0,1:T(2,128)(2,1)S(1)} %broadcast_select_fusion.1), channel_id=1, replica_groups=mesh['farm'=2,'clus'=4,'lag'=4] {'clus'}, dimensions={1}, use_global_device_ids=true | all-gather | bytes 5120 | tf_op jit(solution)/shard_map/all_gather | solution.py:21
  35.4 0.7 dynamic-slice_bitcast_fusion
  36.0 0.2 fusion.1
  36.2 0.0 copy-done.2
  36.2 0.3 fusion.2
  36.5 18.7 %reduce-scatter.3.cloned.1.call-done = f32[32,2048]{1,0:T(8,128)} async-done(((f32[128,2048]{1,0:T(8,128)}), f32[32,2048]{1,0:T(8,128)}) %reduce-scatter.3.cloned.1.call-update) | async-done | bytes 262160 | tf_op jit(solution)/shard_map/reduce_scatter | solution.py:29
  55.2 0.0 reduce-scatter.5.cloned.1.call-update
  55.2 0.1 broadcast_multiply_fusion
  55.3 30.8 %psum.7 = f32[4,256]{1,0:T(4,128)S(1)} all-reduce(f32[4,256]{1,0:T(4,128)S(1)} %broadcast_multiply_fusion), channel_id=1, replica_groups=mesh['farm'=2,'clus'=4,'lag'=4] {'clus','lag'}, use_global_device_ids=true, to_apply=%region_2.3 | all-reduce | flops 1024 | bytes 8192 | tf_op jit(solution)/shard_map/psum | solution.py:33
  86.1 0.4 fusion.4
  86.5 1.7 %fusion = bf16[32,512]{1,0:T(8,128)(2,1)} fusion(f32[32,512]{1,0:T(8,128)} %reduce-scatter.5.cloned.1.call-done, f32[4,512]{1,0:T(4,128)S(1)} %fusion.4, s32[32]{0:T(128)S(1)} %dynamic_slice.10), kind=kOutput, calls=%fused_computation.5 | convolution fusion | flops 819328 | bytes 106624 | tf_op jit(solution)/shard_map/dot_general | solution.py:38
  (10 shorter events, 0.1 us)
Async XLA Ops:
  6.5 79.6 %copy-start = (f32[256,2048]{1,0:T(8,128)S(1)}, f32[256,2048]{1,0:T(8,128)}, u32[]{:S(2)}) copy-start(f32[256,2048]{1,0:T(8,128)} %param.12) | copy-start | bytes 6291460
  6.5 48.7 %reduce-scatter.3.cloned.1.call-start = ((), (), s32[]{:S(2)}) async-start(), calls=%async_computation.3 | async-start | bytes 1310720 | tf_op jit(solution)/shard_map/reduce_scatter | solution.py:29
  9.5 19.3 %copy-start.1 = (s32[8]{0:T(128)S(1)}, s32[8]{0:T(128)}, u32[]{:S(2)}) copy-start(s32[8]{0:T(128)} %param.13) | copy-start | bytes 100
  9.6 19.9 %copy-start.3 = (bf16[8,1,256]{2,0,1:T(8,128)(2,1)S(1)}, bf16[8,1,256]{2,0,1:T(8,128)(2,1)}, u32[]{:S(2)}) copy-start(bf16[8,1,256]{2,0,1:T(8,128)(2,1)} %param.10) | copy-start | bytes 12292
  9.7 20.5 %copy-start.4 = (s32[128]{0:T(128)S(1)}, s32[128]{0:T(128)}, u32[]{:S(2)}) copy-start(s32[128]{0:T(128)} %param.15) | copy-start | bytes 1540
  9.7 26.6 %copy-start.2 = (bf16[1,3,2,256,256]{4,3,2,1,0:T(8,128)(2,1)S(1)}, bf16[1,3,2,256,256]{4,3,2,1,0:T(8,128)(2,1)}, u32[]{:S(2)}) copy-start(bf16[1,3,2,256,256]{4,3,2,1,0:T(8,128)(2,1)} %param.11) | copy-start | bytes 2359300
  28.8 57.7 %reduce-scatter.5.cloned.1.call-start = ((), (), s32[]{:S(2)}) async-start(), calls=%async_computation.4 | async-start | bytes 327680 | tf_op jit(solution)/shard_map/reduce_scatter | solution.py:30
Sparse Core Ops, SparseCore 0:
  28.9 26.2 reduce-scatter.2
  57.8 18.6 reduce-scatter.4
where the time goes:
time: 95.3 us; the launch traced here: 95 us
  blocking collectives  51 us (54%)
  waiting for transfers between devices  18.7 us (20%)
  between operations  13.5 us (14%)
  matrix products  6.47 us (7%)
  local copies, waits for them, and re-layouts  3.53 us (4%)
  other arithmetic  1.76 us (2%)
    psum x1, blocking collectives, shards(): expansion_all = lax.psum(placed, ('clus', 'lag'))  30.8 us
    reduce_scatter x1, waiting for transfers between devices, shards(): lax.psum_scatter(partial_value, 'lag', scatter_dimension=0, tiled=True)  18.7 us
    all_to_all x1, blocking collectives, shards(): lax.all_to_all(picked, 'lag', split_axis=0, concat_axis=1, tiled=True)  15.1 us
    all_gather x1, blocking collectives, shards(): piece = lax.all_gather(wanted, 'clus', axis=1, tiled=True)  5.06 us
    dot_general x1, matrix products, shards(): jnp.einsum('lbp,lpq->bq', arrived, kernel, preferred_element_type=jnp.flo...  3.94 us
  transfers between devices with their start and end apart: 2, of which 1 were waited for; matrix products, arithmetic and copies ran while one was open for 3% of the time, Pallas kernels for 0%

commit v1 on v0

--- a/solution.py
+++ b/solution.py
@@ -1,10 +1,250 @@
+import functools
+
 import jax
 import jax.numpy as jnp
 from jax import lax
+from jax.experimental import pallas as pl
+from jax.experimental.pallas import tpu as pltpu
 from jax.sharding import PartitionSpec as P
 
-
-def shards(history, kernel, moments, coupling, evaluation, offsets, pair_sources, body_cluster):
+MESH = pl.DeviceIdType.MESH
+F32 = jnp.float32
+BF16 = jnp.bfloat16
+
+
+def flipped(index, bits):
+    low, high = lax.rem(index, 2), index // 2
+    if bits & 1:
+        low = 1 - low
+    if bits & 2:
+        high = 1 - high
+    return high * 2 + low
+
+
+def body(
+    lags, clusters,
+    history, kernel, moments, coupling, evaluation, offsets, pair_sources, body_cluster,
+    out,
+    hist, weights, mats, eval_block,
+    own_rows, hist_send, hist_recv,
+    core_send, core_recv, row_send, row_recv, lag_send, lag_recv, kept,
+    moment_all, part_send, part_recv, local_all, far_rows, far,
+    hist_sem, weight_sem, mats_sem, eval_sem,
+    hist_sems, core_sems, row_sems, lag_sems, moment_sems, part_sems, local_sems,
+):
+    farm = lax.axis_index("farm")
+    clus = lax.axis_index("clus")
+    lag = lax.axis_index("lag")
+    bodies, panels = out.shape
+    lags_here = kernel.shape[0]
+    pairs = coupling.shape[1]
+
+    blocks = [flipped(clus, 3), flipped(clus, 2), flipped(clus, 1), clus]
+    hist_in = pltpu.make_async_copy(history, hist, hist_sem)
+    hist_in.start()
+    weights_in = []
+    for quad in range(clusters):
+        columns = pl.ds(pl.multiple_of(blocks[quad] * panels, panels), panels)
+        weights_in.append(
+            pltpu.make_async_copy(
+                kernel.at[:, :, columns], weights.at[quad], weight_sem.at[quad]
+            )
+        )
+        weights_in[quad].start()
+    mats_in = pltpu.make_async_copy(coupling.at[0], mats, mats_sem)
+    mats_in.start()
+    my_columns = pl.ds(pl.multiple_of(clus * panels, panels), panels)
+    eval_in = pltpu.make_async_copy(evaluation.at[:, my_columns], eval_block, eval_sem)
+    eval_in.start()
+
+    lag_peers = [(farm, clus, flipped(lag, j)) for j in range(lags)]
+    clus_peers = [(farm, flipped(clus, r), lag) for r in range(clusters)]
+    barrier = pltpu.get_barrier_semaphore()
+    for peer in lag_peers[1:] + clus_peers[1:]:
+        pl.semaphore_signal(barrier, inc=1, device_id=peer, device_id_type=MESH)
+
+    for slot in range(moments.shape[0]):
+        moment_all[clus, slot : slot + 1, :] = moments[slot].astype(F32)
+    hist_in.wait()
+    for l in range(lags_here):
+        own_rows[l] = hist[offsets[lag * lags_here + l]]
+        for j in range(1, lags):
+            hist_send[j - 1, l] = hist[offsets[lag_peers[j][2] * lags_here + l]]
+    pl.semaphore_wait(barrier, lags - 1 + clusters - 1)
+
+    sent = []
+
+    def send(src, dst, sems, at, peer):
+        copy = pltpu.make_async_remote_copy(
+            src_ref=src, dst_ref=dst,
+            send_sem=sems.at[(0,) + at], recv_sem=sems.at[(1,) + at],
+            device_id=peer, device_id_type=MESH,
+        )
+        copy.start()
+        sent.append(copy)
+        return copy
+
+    hist_copies = [
+        send(hist_send.at[j - 1], hist_recv.at[j - 1], hist_sems, (j - 1,), lag_peers[j])
+        for j in range(1, lags)
+    ]
+    moment_copies = [
+        send(moment_all.at[clus], moment_all.at[clus], moment_sems, (r - 1,), clus_peers[r])
+        for r in range(1, clusters)
+    ]
+
+    core_copies, row_copies, lag_copies = {}, {}, []
+
+    def product(j, quad):
+        rows = own_rows if j == 0 else hist_recv.at[j - 1]
+        total = None
+        for l in range(lags_here):
+            term = jnp.dot(rows[l], weights[quad, l], preferred_element_type=F32)
+            total = term if total is None else total + term
+        return total
+
+    def begin(j):
+        if j > 0:
+            hist_copies[j - 1].wait_recv()
+        for side, quad in ((0, 0), (1, 2)):
+            if j == 0:
+                weights_in[quad].wait()
+            core_send[j, side] = product(j, quad)
+            core_copies[j, side] = send(
+                core_send.at[j, side], core_recv.at[j, side], core_sems, (j, side), clus_peers[1]
+            )
+        if j == 0:
+            weights_in[1].wait()
+        other = product(j, 1)
+        core_copies[j, 0].wait_recv()
+        row_send[j] = other + core_recv[j, 0]
+        row_copies[j] = send(row_send.at[j], row_recv.at[j], row_sems, (j,), clus_peers[2])
+        if j == 0:
+            weights_in[3].wait()
+        mine = product(j, 3)
+        core_copies[j, 1].wait_recv()
+        kept[j] = mine + core_recv[j, 1]
+
+    def finish(j):
+        row_copies[j].wait_recv()
+        if j == 0:
+            kept[0] = kept[0] + row_recv[0]
+        else:
+            lag_send[j - 1] = kept[j] + row_recv[j]
+            lag_copies.append(
+                send(lag_send.at[j - 1], lag_recv.at[j - 1], lag_sems, (j - 1,), lag_peers[j])
+            )
+
+    begin(0)
+
+    mats_in.wait()
+    for copy in moment_copies:
+        copy.wait_recv()
+    part = None
+    for l in range(lags_here):
+        slot = offsets[lag * lags_here + l]
+        for k in range(pairs):
+            row = moment_all[pair_sources[clus, k], pl.ds(slot, 1), :]
+            row = jnp.broadcast_to(row, (16, row.shape[1])).astype(BF16)
+            term = lax.dot_general(
+                row, mats[k, l], (((1,), (1,)), ((), ())), preferred_element_type=F32
+            )
+            part = term if part is None else part + term
+    part_send[...] = part[0:8]
+    part_copies = [
+        send(part_send, part_recv.at[j - 1], part_sems, (j - 1,), lag_peers[j])
+        for j in range(1, lags)
+    ]
+
+    begin(1)
+    finish(0)
+
+    local = part_send[...]
+    for j in range(1, lags):
+        part_copies[j - 1].wait_recv()
+        local = local + part_recv[j - 1]
+    local_all[clus] = local
+    local_copies = [
+        send(local_all.at[clus], local_all.at[clus], local_sems, (r - 1,), clus_peers[r])
+        for r in range(1, clusters)
+    ]
+
+    begin(2)
+    finish(1)
+    begin(3)
+    finish(2)
+
+    eval_in.wait()
+    for copy in local_copies:
+        copy.wait_recv()
+    expansions = local_all[...].reshape(clusters * 8, local_all.shape[2])
+    far_rows[...] = jnp.dot(
+        expansions, eval_block[...], precision=lax.Precision.HIGHEST, preferred_element_type=F32
+    )
+    for b in range(bodies):
+        far[b : b + 1, :] = far_rows[pl.ds(body_cluster[lag * bodies + b] * 8, 1), :]
+
+    finish(3)
+    total = kept[0]
+    for j in range(1, lags):
+        lag_copies[j - 1].wait_recv()
+        total = total + lag_recv[j - 1]
+    out[...] = (total + far[...]).astype(BF16)
+    for copy in sent:
+        copy.wait_send()
+
+
+def shards_kernel(lags, clusters, history, kernel, moments, coupling, evaluation, offsets, pair_sources, body_cluster):
+    slots, bodies, panels = history.shape
+    lags_here, depth, _ = kernel.shape
+    terms = moments.shape[2]
+    pairs = coupling.shape[1]
+    dma = pltpu.SemaphoreType.DMA
+    anywhere = pl.BlockSpec(memory_space=pl.ANY)
+    vmem = pl.BlockSpec(memory_space=pltpu.VMEM)
+    smem = pl.BlockSpec(memory_space=pltpu.SMEM)
+    block = (bodies, panels)
+    flops = 2 * lags * bodies * lags_here * depth * clusters * panels
+    return pl.pallas_call(
+        functools.partial(body, lags, clusters),
+        out_shape=jax.ShapeDtypeStruct(block, BF16),
+        in_specs=[anywhere, anywhere, vmem, anywhere, anywhere, smem, smem, smem],
+        out_specs=vmem,
+        scratch_shapes=[
+            pltpu.VMEM((slots,) + block, BF16),
+            pltpu.VMEM((clusters, lags_here, depth, panels), BF16),
+            pltpu.VMEM((pairs, lags_here, terms, terms), BF16),
+            pltpu.VMEM((terms, panels), F32),
+            pltpu.VMEM((lags_here,) + block, BF16),
+            pltpu.VMEM((lags - 1, lags_here) + block, BF16),
+            pltpu.VMEM((lags - 1, lags_here) + block, BF16),
+            pltpu.VMEM((lags, 2) + block, F32),
+            pltpu.VMEM((lags, 2) + block, F32),
+            pltpu.VMEM((lags,) + block, F32),
+            pltpu.VMEM((lags,) + block, F32),
+            pltpu.VMEM((lags - 1,) + block, F32),
+            pltpu.VMEM((lags - 1,) + block, F32),
+            pltpu.VMEM((lags,) + block, F32),
+            pltpu.VMEM((clusters, slots, terms), F32),
+            pltpu.VMEM((8, terms), F32),
+            pltpu.VMEM((lags - 1, 8, terms), F32),
+            pltpu.VMEM((clusters, 8, terms), F32),
+            pltpu.VMEM((clusters * 8, panels), F32),
+            pltpu.VMEM(block, F32),
+            dma, dma((clusters,)), dma, dma,
+            dma((2, lags - 1)), dma((2, lags, 2)), dma((2, lags)), dma((2, lags - 1)),
+            dma((2, clusters - 1)), dma((2, lags - 1)), dma((2, clusters - 1)),
+        ],
+        compiler_params=pltpu.CompilerParams(
+            collective_id=0, has_side_effects=True, vmem_limit_bytes=48 * 1024 * 1024
+        ),
+        cost_estimate=pl.CostEstimate(
+            flops=flops, bytes_accessed=2 * kernel.size, transcendentals=0
+        ),
+    )(history, kernel, moments, coupling, evaluation, offsets, pair_sources, body_cluster)
+
+
+def shards_general(history, kernel, moments, coupling, evaluation, offsets, pair_sources, body_cluster):
     lag_index = lax.axis_index("lag")
     clus_index = lax.axis_index("clus")
     clus_count = lax.axis_size("clus")
@@ -51,4 +291,9 @@
         P(),
     )
     out_specs = P(("farm", "lag"), "clus")
+    lags, clusters = mesh.shape["lag"], mesh.shape["clus"]
+    if lags == 4 and clusters == 4:
+        shards = functools.partial(shards_kernel, lags, clusters)
+    else:
+        shards = shards_general
     return jax.shard_map(shards, mesh=mesh, in_specs=in_specs, out_specs=out_specs, check_vma=False)

time: 95.3 us -> 33.4 us (0.35)
  blocking collectives: 51 us -> 0 us
  Pallas kernels: 0 us -> 26.2 us
  waiting for transfers between devices: 18.7 us -> 0 us
  between operations: 13.5 us -> 0.02 us
  matrix products: 6.47 us -> 0 us
  local copies, waits for them, and re-layouts: 3.53 us -> 6.97 us
  other arithmetic: 1.76 us -> 0 us
    psum x1 -> x0, blocking collectives: 30.8 us -> none  [shards(): expansion_all = lax.psum(placed, ('clus', 'lag'))]
    pallas_call x0 -> x1, Pallas kernels: none -> 26.2 us  [shards_kernel(): pl.pallas_call(functools.partial(body, lags, clusters), out_shape=jax.Sha...]
    reduce_scatter x2 -> x0, waiting for transfers between devices: 18.7 us -> none  [the longest x1 18.7 us: shards(): lax.psum_scatter(partial_value, 'lag', scatter_dimension=0, tiled=True)]
    all_to_all x1 -> x0, blocking collectives: 15.1 us -> none  [shards(): lax.all_to_all(picked, 'lag', split_axis=0, concat_axis=1, tiled=True)]
    unnamed x10 -> x14, local copies, waits for them, and re-layouts: 0.03 us -> 6.97 us
    dot_general x5 -> x0, matrix products: 6.47 us -> none  [the longest x1 3.94 us: shards(): jnp.einsum('lbp,lpq->bq', arrived, kernel, preferred_element_type=jnp.flo...]
    all_gather x1 -> x0, blocking collectives: 5.06 us -> none  [shards(): piece = lax.all_gather(wanted, 'clus', axis=1, tiled=True)]
    gather x3 -> x0, local copies, waits for them, and re-layouts: 2.72 us -> none  [the longest x1 1.51 us: shards(): picked = jnp.take(history, offsets, axis=0)]
  transfers between devices with their start and end apart: 2 -> 0, of which waited for: 1 -> 0; matrix products, arithmetic and copies ran while one was open for 3% -> 0% of each run, Pallas kernels for 0% -> 0%
where the time goes in v1:
time: 33.4 us; the launch traced here: 33.1 us
  Pallas kernels  26.2 us (78%)
  local copies, waits for them, and re-layouts  6.97 us (21%)
    pallas_call x1, Pallas kernels, shards_kernel(): pl.pallas_call(functools.partial(body, lags, clusters), out_shape=jax.Sha...  26.2 us
    unnamed x14, local copies, waits for them, and re-layouts  6.97 us

profile of v1, /device:TPU:0, one launch (start us, length us, event | category | flops | bytes accessed | tf_op | source)
XLA Modules:
  0.0 33.1 jit_solution(5018501573879898268)
XLA Ops:
  0.0 0.7 %copy.9.moments = bf16[8,1,256]{2,1,0:T(2,128)(2,1)S(1)} copy(bf16[8,1,256]{2,0,1:T(8,128)(2,1)} %param.10) | data formatting | bytes 8192 | tf_op args[2]
  0.7 0.0 copy-start
  0.7 1.6 %copy-done = f32[256,2048]{1,0:T(8,128)S(1)} copy-done((f32[256,2048]{1,0:T(8,128)S(1)}, f32[256,2048]{1,0:T(8,128)}, u32[]{:S(2)}) %copy-start) | copy-done | bytes 2097176
  2.3 0.0 copy-start.1
  2.3 1.1 %copy-done.1 = bf16[1,3,2,256,256]{4,3,2,1,0:T(8,128)(2,1)S(1)} copy-done((bf16[1,3,2,256,256]{4,3,2,1,0:T(8,128)(2,1)S(1)}, bf16[1,3,2,256,256]{4,3,2,1,0:T(8,128)(2,1)}, u32[]{:S(2)}) %copy-start.1) | copy-done | bytes 786456
  3.4 0.0 copy-start.2
  3.4 0.9 %copy-done.2 = bf16[8,32,512]{2,1,0:T(8,128)(2,1)S(1)} copy-done((bf16[8,32,512]{2,1,0:T(8,128)(2,1)S(1)}, bf16[8,32,512]{2,1,0:T(8,128)(2,1)}, u32[]{:S(2)}) %copy-start.2) | copy-done | bytes 262168
  4.4 0.0 copy-start.3
  4.4 0.7 %copy-done.3 = s32[4,3]{1,0:T(4,128)S(1)} copy-done((s32[4,3]{1,0:T(4,128)S(1)}, s32[4,3]{1,0:T(4,128)}, u32[]{:S(2)}) %copy-start.3) | copy-done | bytes 72
  5.1 0.0 copy-start.4
  5.1 0.7 %copy-done.4 = s32[8]{0:T(128)S(1)} copy-done((s32[8]{0:T(128)S(1)}, s32[8]{0:T(128)}, u32[]{:S(2)}) %copy-start.4) | copy-done | bytes 56
  5.7 0.0 copy-start.5
  5.7 0.7 %copy-done.5 = s32[128]{0:T(128)S(1)} copy-done((s32[128]{0:T(128)S(1)}, s32[128]{0:T(128)}, u32[]{:S(2)}) %copy-start.5) | copy-done | bytes 536
  6.4 26.2 %shard_map.82 = bf16[32,512]{1,0:T(8,128)(2,1)S(1)} custom-call(bf16[8,32,512]{2,1,0:T(8,128)(2,1)S(1)} %copy-done.2, bf16[2,512,2048]{2,1,0:T(8,128)(2,1)} %kernel.1, bf16[8,1,256]{2,1,0:T(2,128)(2,1)S(1)} %copy.9.moments, bf16[1,3,2,256,256]{4,3,2,1,0:T(8,128)(2,1)S(1)} %copy-done.1, f32[256,2048]{1,0:T(8,128)S(1)} %copy-done, s32[8]{0:T(128)S(1)} %copy-done.4, ...), custom_call_target="tpu_custom_call" | custom-call | flops 536870912 | bytes 4194304 | tf_op jit(solution)/shard_map/pallas_call | solution.py:208
  32.5 0.6 %copy.11 = bf16[32,512]{1,0:T(8,128)(2,1)} copy(bf16[32,512]{1,0:T(8,128)(2,1)S(1)} %shard_map.82) | data formatting | bytes 65536
Async XLA Ops:
  0.7 1.6 %copy-start = (f32[256,2048]{1,0:T(8,128)S(1)}, f32[256,2048]{1,0:T(8,128)}, u32[]{:S(2)}) copy-start(f32[256,2048]{1,0:T(8,128)} %evaluation.1) | copy-start | bytes 6291460
  2.3 1.1 %copy-start.1 = (bf16[1,3,2,256,256]{4,3,2,1,0:T(8,128)(2,1)S(1)}, bf16[1,3,2,256,256]{4,3,2,1,0:T(8,128)(2,1)}, u32[]{:S(2)}) copy-start(bf16[1,3,2,256,256]{4,3,2,1,0:T(8,128)(2,1)} %coupling.1) | copy-start | bytes 2359300
  3.4 0.9 %copy-start.2 = (bf16[8,32,512]{2,1,0:T(8,128)(2,1)S(1)}, bf16[8,32,512]{2,1,0:T(8,128)(2,1)}, u32[]{:S(2)}) copy-start(bf16[8,32,512]{2,1,0:T(8,128)(2,1)} %history.1) | copy-start | bytes 786436
  4.4 0.7 %copy-start.3 = (s32[4,3]{1,0:T(4,128)S(1)}, s32[4,3]{1,0:T(4,128)}, u32[]{:S(2)}) copy-start(s32[4,3]{1,0:T(4,128)} %pair_sources.1) | copy-start | bytes 148
  5.1 0.7 %copy-start.4 = (s32[8]{0:T(128)S(1)}, s32[8]{0:T(128)}, u32[]{:S(2)}) copy-start(s32[8]{0:T(128)} %offsets.1) | copy-start | bytes 100
  5.7 0.7 %copy-start.5 = (s32[128]{0:T(128)S(1)}, s32[128]{0:T(128)}, u32[]{:S(2)}) copy-start(s32[128]{0:T(128)} %body_cluster.1) | copy-start | bytes 1540

commit v2 on v1

--- a/solution.py
+++ b/solution.py
@@ -63,8 +63,7 @@
     for peer in lag_peers[1:] + clus_peers[1:]:
         pl.semaphore_signal(barrier, inc=1, device_id=peer, device_id_type=MESH)
 
-    for slot in range(moments.shape[0]):
-        moment_all[clus, slot : slot + 1, :] = moments[slot].astype(F32)
+    moment_all[clus] = moments[...].astype(F32)
     hist_in.wait()
     for l in range(lags_here):
         own_rows[l] = hist[offsets[lag * lags_here + l]]
@@ -198,6 +197,7 @@
     slots, bodies, panels = history.shape
     lags_here, depth, _ = kernel.shape
     terms = moments.shape[2]
+    moments = moments.reshape(slots, terms)
     pairs = coupling.shape[1]
     dma = pltpu.SemaphoreType.DMA
     anywhere = pl.BlockSpec(memory_space=pl.ANY)
@@ -236,7 +236,7 @@
             dma((2, clusters - 1)), dma((2, lags - 1)), dma((2, clusters - 1)),
         ],
         compiler_params=pltpu.CompilerParams(
-            collective_id=0, has_side_effects=True, vmem_limit_bytes=48 * 1024 * 1024
+            collective_id=0, has_side_effects=True, vmem_limit_bytes=63 * 1024 * 1024
         ),
         cost_estimate=pl.CostEstimate(
             flops=flops, bytes_accessed=2 * kernel.size, transcendentals=0

time: 33.4 us -> 28.5 us (0.85)
  local copies, waits for them, and re-layouts: 6.97 us -> 1.38 us
  Pallas kernels: 26.2 us -> 26.9 us
    unnamed x14 -> x1, local copies, waits for them, and re-layouts: 6.97 us -> 1.38 us
    pallas_call x1, Pallas kernels: 26.2 us -> 26.9 us  [shards_kernel(): pl.pallas_call(functools.partial(body, lags, clusters), out_shape=jax.Sha...]
where the time goes in v2:
time: 28.5 us; the launch traced here: 28.3 us
  Pallas kernels  26.9 us (94%)
  local copies, waits for them, and re-layouts  1.38 us (5%)
    pallas_call x1, Pallas kernels, shards_kernel(): pl.pallas_call(functools.partial(body, lags, clusters), out_shape=jax.Sha...  26.9 us
    unnamed x1, local copies, waits for them, and re-layouts  1.38 us

profile of v2, /device:TPU:0, one launch (start us, length us, event | category | flops | bytes accessed | tf_op | source)
XLA Modules:
  0.0 28.3 jit_solution(954104810186688942)
XLA Ops:
  0.0 26.9 %shard_map.82 = bf16[32,512]{1,0:T(8,128)(2,1)} custom-call(bf16[8,32,512]{2,1,0:T(8,128)(2,1)} %history.1, bf16[2,512,2048]{2,1,0:T(8,128)(2,1)} %kernel.1, bf16[8,256]{1,0:T(8,128)(2,1)} %bitcast.1, bf16[1,3,2,256,256]{4,3,2,1,0:T(8,128)(2,1)} %coupling.1, f32[256,2048]{1,0:T(8,128)} %evaluation.1, s32[8]{0:T(128)} %offsets.1, s32[4,3]{1,0:T(4,128)} %pair_sources.1, ...), custom_call_target="tpu_custom_call" | custom-call | flops 536870912 | bytes 4194304 | tf_op jit(solution)/shard_map/pallas_call | solution.py:208
  26.9 1.4 %copy.10 = bf16[32,512]{1,0:T(8,128)(2,1)} copy(bf16[32,512]{1,0:T(8,128)(2,1)} %shard_map.82) | data formatting | bytes 65536

commit v3 on v2

--- a/solution.py
+++ b/solution.py
@@ -21,16 +21,39 @@
     return high * 2 + low
 
 
+def spread(tile, shape):
+    column = jnp.concatenate([tile] * (shape[0] // 8), axis=0)
+    return jnp.concatenate([column] * (shape[1] // 128), axis=1)
+
+
+def encode(values, codes, scales):
+    rows, columns = values.shape
+    size = jnp.abs(values)
+    peak = None
+    for i in range(rows // 8):
+        for j in range(columns // 128):
+            part = size[8 * i : 8 * i + 8, 128 * j : 128 * j + 128]
+            peak = part if peak is None else jnp.maximum(peak, part)
+    peak = jnp.maximum(peak, 1e-33)
+    scales[...] = peak * (1.0 / 32767.0)
+    scaled = jnp.round(values * spread(32767.0 / peak, values.shape))
+    codes[...] = scaled.astype(jnp.int32).astype(jnp.int16)
+
+
+def decode(codes, scales):
+    return codes[...].astype(jnp.int32).astype(F32) * spread(scales[...], codes.shape)
+
+
 def body(
     lags, clusters,
     history, kernel, moments, coupling, evaluation, offsets, pair_sources, body_cluster,
     out,
     hist, weights, mats, eval_block,
     own_rows, hist_send, hist_recv,
-    core_send, core_recv, row_send, row_recv, lag_send, lag_recv, kept,
+    core_send, core_recv, row_send, row_recv, row_scale, row_scaled, lag_send, lag_recv, lag_scale, lag_scaled, kept,
     moment_all, part_send, part_recv, local_all, far_rows, far,
     hist_sem, weight_sem, mats_sem, eval_sem,
-    hist_sems, core_sems, row_sems, lag_sems, moment_sems, part_sems, local_sems,
+    hist_sems, core_sems, row_sems, lag_sems, row_scale_sems, lag_scale_sems, moment_sems, part_sems, local_sems,
 ):
     farm = lax.axis_index("farm")
     clus = lax.axis_index("clus")
@@ -83,16 +106,17 @@
         sent.append(copy)
         return copy
 
-    hist_copies = [
-        send(hist_send.at[j - 1], hist_recv.at[j - 1], hist_sems, (j - 1,), lag_peers[j])
-        for j in range(1, lags)
-    ]
+    def send_history(j):
+        return send(hist_send.at[j - 1], hist_recv.at[j - 1], hist_sems, (j - 1,), lag_peers[j])
+
+    hist_copies = {j: send_history(j) for j in (2, 1)}
     moment_copies = [
         send(moment_all.at[clus], moment_all.at[clus], moment_sems, (r - 1,), clus_peers[r])
         for r in range(1, clusters)
     ]
 
-    core_copies, row_copies, lag_copies = {}, {}, []
+    hist_copies[3] = send_history(3)
+    core_copies, row_copies, lag_copies = {}, {}, {}
 
     def product(j, quad):
         rows = own_rows if j == 0 else hist_recv.at[j - 1]
@@ -104,7 +128,7 @@
 
     def begin(j):
         if j > 0:
-            hist_copies[j - 1].wait_recv()
+            hist_copies[j].wait_recv()
         for side, quad in ((0, 0), (1, 2)):
             if j == 0:
                 weights_in[quad].wait()
@@ -116,8 +140,11 @@
             weights_in[1].wait()
         other = product(j, 1)
         core_copies[j, 0].wait_recv()
-        row_send[j] = other + core_recv[j, 0]
-        row_copies[j] = send(row_send.at[j], row_recv.at[j], row_sems, (j,), clus_peers[2])
+        encode(other + core_recv[j, 0], row_send.at[j], row_scale.at[j])
+        row_copies[j] = (
+            send(row_send.at[j], row_recv.at[j], row_sems, (j,), clus_peers[2]),
+            send(row_scale.at[j], row_scaled.at[j], row_scale_sems, (j,), clus_peers[2]),
+        )
         if j == 0:
             weights_in[3].wait()
         mine = product(j, 3)
@@ -125,13 +152,17 @@
         kept[j] = mine + core_recv[j, 1]
 
     def finish(j):
-        row_copies[j].wait_recv()
+        for copy in row_copies[j]:
+            copy.wait_recv()
+        total = kept[j] + decode(row_recv.at[j], row_scaled.at[j])
         if j == 0:
-            kept[0] = kept[0] + row_recv[0]
+            kept[0] = total
         else:
-            lag_send[j - 1] = kept[j] + row_recv[j]
-            lag_copies.append(
-                send(lag_send.at[j - 1], lag_recv.at[j - 1], lag_sems, (j - 1,), lag_peers[j])
+            i = j - 1
+            encode(total, lag_send.at[i], lag_scale.at[i])
+            lag_copies[j] = (
+                send(lag_send.at[i], lag_recv.at[i], lag_sems, (i,), lag_peers[j]),
+                send(lag_scale.at[i], lag_scaled.at[i], lag_scale_sems, (i,), lag_peers[j]),
             )
 
     begin(0)
@@ -170,8 +201,6 @@
 
     begin(2)
     finish(1)
-    begin(3)
-    finish(2)
 
     eval_in.wait()
     for copy in local_copies:
@@ -183,11 +212,14 @@
     for b in range(bodies):
         far[b : b + 1, :] = far_rows[pl.ds(body_cluster[lag * bodies + b] * 8, 1), :]
 
+    finish(2)
+    begin(3)
     finish(3)
     total = kept[0]
     for j in range(1, lags):
-        lag_copies[j - 1].wait_recv()
-        total = total + lag_recv[j - 1]
+        for copy in lag_copies[j]:
+            copy.wait_recv()
+        total = total + decode(lag_recv.at[j - 1], lag_scaled.at[j - 1])
     out[...] = (total + far[...]).astype(BF16)
     for copy in sent:
         copy.wait_send()
@@ -220,10 +252,14 @@
             pltpu.VMEM((lags - 1, lags_here) + block, BF16),
             pltpu.VMEM((lags, 2) + block, F32),
             pltpu.VMEM((lags, 2) + block, F32),
-            pltpu.VMEM((lags,) + block, F32),
-            pltpu.VMEM((lags,) + block, F32),
-            pltpu.VMEM((lags - 1,) + block, F32),
-            pltpu.VMEM((lags - 1,) + block, F32),
+            pltpu.VMEM((lags,) + block, jnp.int16),
+            pltpu.VMEM((lags,) + block, jnp.int16),
+            pltpu.VMEM((lags, 8, 128), F32),
+            pltpu.VMEM((lags, 8, 128), F32),
+            pltpu.VMEM((lags - 1,) + block, jnp.int16),
+            pltpu.VMEM((lags - 1,) + block, jnp.int16),
+            pltpu.VMEM((lags - 1, 8, 128), F32),
+            pltpu.VMEM((lags - 1, 8, 128), F32),
             pltpu.VMEM((lags,) + block, F32),
             pltpu.VMEM((clusters, slots, terms), F32),
             pltpu.VMEM((8, terms), F32),
@@ -233,6 +269,7 @@
             pltpu.VMEM(block, F32),
             dma, dma((clusters,)), dma, dma,
             dma((2, lags - 1)), dma((2, lags, 2)), dma((2, lags)), dma((2, lags - 1)),
+            dma((2, lags)), dma((2, lags - 1)),
             dma((2, clusters - 1)), dma((2, lags - 1)), dma((2, clusters - 1)),
         ],
         compiler_params=pltpu.CompilerParams(

time: 28.5 us -> 29.1 us (1.021)
  Pallas kernels: 26.9 us -> 27.5 us
    pallas_call x1, Pallas kernels: 26.9 us -> 27.5 us  [shards_kernel(): pl.pallas_call(functools.partial(body, lags, clusters), out_shape=jax.Sha...]
where the time goes in v3:
time: 29.1 us; the launch traced here: 28.9 us
  Pallas kernels  27.5 us (95%)
  local copies, waits for them, and re-layouts  1.38 us (5%)
    pallas_call x1, Pallas kernels, shards_kernel(): pl.pallas_call(functools.partial(body, lags, clusters), out_shape=jax.Sha...  27.5 us
    unnamed x1, local copies, waits for them, and re-layouts  1.38 us

profile of v3, /device:TPU:0, one launch (start us, length us, event | category | flops | bytes accessed | tf_op | source)
XLA Modules:
  0.0 28.9 jit_solution(12526510250725622668)
XLA Ops:
  0.0 27.5 %shard_map.82 = bf16[32,512]{1,0:T(8,128)(2,1)} custom-call(bf16[8,32,512]{2,1,0:T(8,128)(2,1)} %history.1, bf16[2,512,2048]{2,1,0:T(8,128)(2,1)} %kernel.1, bf16[8,256]{1,0:T(8,128)(2,1)} %bitcast.1, bf16[1,3,2,256,256]{4,3,2,1,0:T(8,128)(2,1)} %coupling.1, f32[256,2048]{1,0:T(8,128)} %evaluation.1, s32[8]{0:T(128)} %offsets.1, s32[4,3]{1,0:T(4,128)} %pair_sources.1, ...), custom_call_target="tpu_custom_call" | custom-call | flops 536870912 | bytes 4194304 | tf_op jit(solution)/shard_map/pallas_call | solution.py:240
  27.5 1.4 %copy.10 = bf16[32,512]{1,0:T(8,128)(2,1)} copy(bf16[32,512]{1,0:T(8,128)(2,1)} %shard_map.82) | data formatting | bytes 65536

commit v4 on v3

--- a/solution.py
+++ b/solution.py
@@ -49,7 +49,7 @@
     history, kernel, moments, coupling, evaluation, offsets, pair_sources, body_cluster,
     out,
     hist, weights, mats, eval_block,
-    own_rows, hist_send, hist_recv,
+    rows, hist_send,
     core_send, core_recv, row_send, row_recv, row_scale, row_scaled, lag_send, lag_recv, lag_scale, lag_scaled, kept,
     moment_all, part_send, part_recv, local_all, far_rows, far,
     hist_sem, weight_sem, mats_sem, eval_sem,
@@ -89,7 +89,7 @@
     moment_all[clus] = moments[...].astype(F32)
     hist_in.wait()
     for l in range(lags_here):
-        own_rows[l] = hist[offsets[lag * lags_here + l]]
+        rows[l, 0:bodies] = hist[offsets[lag * lags_here + l]]
         for j in range(1, lags):
             hist_send[j - 1, l] = hist[offsets[lag_peers[j][2] * lags_here + l]]
     pl.semaphore_wait(barrier, lags - 1 + clusters - 1)
@@ -107,7 +107,8 @@
         return copy
 
     def send_history(j):
-        return send(hist_send.at[j - 1], hist_recv.at[j - 1], hist_sems, (j - 1,), lag_peers[j])
+        landing = rows.at[:, pl.ds(j * bodies, bodies)]
+        return send(hist_send.at[j - 1], landing, hist_sems, (j - 1,), lag_peers[j])
 
     hist_copies = {j: send_history(j) for j in (2, 1)}
     moment_copies = [
@@ -118,54 +119,55 @@
     hist_copies[3] = send_history(3)
     core_copies, row_copies, lag_copies = {}, {}, {}
 
-    def product(j, quad):
-        rows = own_rows if j == 0 else hist_recv.at[j - 1]
+    height = 2 * bodies
+
+    def product(group, quad):
+        if group == 0:
+            weights_in[quad].wait()
         total = None
         for l in range(lags_here):
-            term = jnp.dot(rows[l], weights[quad, l], preferred_element_type=F32)
+            term = jnp.dot(
+                rows[l, group * height : (group + 1) * height], weights[quad, l],
+                preferred_element_type=F32,
+            )
             total = term if total is None else total + term
         return total
 
-    def begin(j):
-        if j > 0:
-            hist_copies[j].wait_recv()
+    def begin(group):
+        for j in (2 * group, 2 * group + 1):
+            if j > 0:
+                hist_copies[j].wait_recv()
         for side, quad in ((0, 0), (1, 2)):
-            if j == 0:
-                weights_in[quad].wait()
-            core_send[j, side] = product(j, quad)
-            core_copies[j, side] = send(
-                core_send.at[j, side], core_recv.at[j, side], core_sems, (j, side), clus_peers[1]
+            core_send[group, side] = product(group, quad)
+            core_copies[group, side] = send(
+                core_send.at[group, side], core_recv.at[group, side],
+                core_sems, (group, side), clus_peers[1],
             )
-        if j == 0:
-            weights_in[1].wait()
-        other = product(j, 1)
-        core_copies[j, 0].wait_recv()
-        encode(other + core_recv[j, 0], row_send.at[j], row_scale.at[j])
-        row_copies[j] = (
-            send(row_send.at[j], row_recv.at[j], row_sems, (j,), clus_peers[2]),
-            send(row_scale.at[j], row_scaled.at[j], row_scale_sems, (j,), clus_peers[2]),
+        other = product(group, 1)
+        core_copies[group, 0].wait_recv()
+        encode(other + core_recv[group, 0], row_send.at[group], row_scale.at[group])
+        row_copies[group] = (
+            send(row_send.at[group], row_recv.at[group], row_sems, (group,), clus_peers[2]),
+            send(row_scale.at[group], row_scaled.at[group], row_scale_sems, (group,), clus_peers[2]),
         )
-        if j == 0:
-            weights_in[3].wait()
-        mine = product(j, 3)
-        core_copies[j, 1].wait_recv()
-        kept[j] = mine + core_recv[j, 1]
-
-    def finish(j):
-        for copy in row_copies[j]:
+        mine = product(group, 3)
+        core_copies[group, 1].wait_recv()
+        kept[group] = mine + core_recv[group, 1]
+
+    def finish(group):
+        for copy in row_copies[group]:
             copy.wait_recv()
-        total = kept[j] + decode(row_recv.at[j], row_scaled.at[j])
-        if j == 0:
+        total = kept[group] + decode(row_recv.at[group], row_scaled.at[group])
+        if group == 0:
             kept[0] = total
-        else:
-            i = j - 1
-            encode(total, lag_send.at[i], lag_scale.at[i])
-            lag_copies[j] = (
-                send(lag_send.at[i], lag_recv.at[i], lag_sems, (i,), lag_peers[j]),
-                send(lag_scale.at[i], lag_scaled.at[i], lag_scale_sems, (i,), lag_peers[j]),
-            )
-
-    begin(0)
+        for j in (2 * group, 2 * group + 1):
+            if j > 0:
+                i, top = j - 1, (j - 2 * group) * bodies
+                encode(total[top : top + bodies], lag_send.at[i], lag_scale.at[i])
+                lag_copies[j] = (
+                    send(lag_send.at[i], lag_recv.at[i], lag_sems, (i,), lag_peers[j]),
+                    send(lag_scale.at[i], lag_scaled.at[i], lag_scale_sems, (i,), lag_peers[j]),
+                )
 
     mats_in.wait()
     for copy in moment_copies:
@@ -186,8 +188,7 @@
         for j in range(1, lags)
     ]
 
-    begin(1)
-    finish(0)
+    begin(0)
 
     local = part_send[...]
     for j in range(1, lags):
@@ -199,8 +200,7 @@
         for r in range(1, clusters)
     ]
 
-    begin(2)
-    finish(1)
+    finish(0)
 
     eval_in.wait()
     for copy in local_copies:
@@ -212,10 +212,9 @@
     for b in range(bodies):
         far[b : b + 1, :] = far_rows[pl.ds(body_cluster[lag * bodies + b] * 8, 1), :]
 
-    finish(2)
-    begin(3)
-    finish(3)
-    total = kept[0]
+    begin(1)
+    finish(1)
+    total = kept[0, 0:bodies]
     for j in range(1, lags):
         for copy in lag_copies[j]:
             copy.wait_recv()
@@ -235,11 +234,11 @@
     anywhere = pl.BlockSpec(memory_space=pl.ANY)
     vmem = pl.BlockSpec(memory_space=pltpu.VMEM)
     smem = pl.BlockSpec(memory_space=pltpu.SMEM)
-    block = (bodies, panels)
+    block, double, groups = (bodies, panels), (2 * bodies, panels), lags // 2
     flops = 2 * lags * bodies * lags_here * depth * clusters * panels
     return pl.pallas_call(
         functools.partial(body, lags, clusters),
-        out_shape=jax.ShapeDtypeStruct(block, BF16),
+        out_shape=pltpu.VMEM(block, BF16),
         in_specs=[anywhere, anywhere, vmem, anywhere, anywhere, smem, smem, smem],
         out_specs=vmem,
         scratch_shapes=[
@@ -247,20 +246,19 @@
             pltpu.VMEM((clusters, lags_here, depth, panels), BF16),
             pltpu.VMEM((pairs, lags_here, terms, terms), BF16),
             pltpu.VMEM((terms, panels), F32),
-            pltpu.VMEM((lags_here,) + block, BF16),
+            pltpu.VMEM((lags_here, lags * bodies, panels), BF16),
             pltpu.VMEM((lags - 1, lags_here) + block, BF16),
-            pltpu.VMEM((lags - 1, lags_here) + block, BF16),
-            pltpu.VMEM((lags, 2) + block, F32),
-            pltpu.VMEM((lags, 2) + block, F32),
-            pltpu.VMEM((lags,) + block, jnp.int16),
-            pltpu.VMEM((lags,) + block, jnp.int16),
-            pltpu.VMEM((lags, 8, 128), F32),
-            pltpu.VMEM((lags, 8, 128), F32),
+            pltpu.VMEM((groups, 2) + double, F32),
+            pltpu.VMEM((groups, 2) + double, F32),
+            pltpu.VMEM((groups,) + double, jnp.int16),
+            pltpu.VMEM((groups,) + double, jnp.int16),
+            pltpu.VMEM((groups, 8, 128), F32),
+            pltpu.VMEM((groups, 8, 128), F32),
             pltpu.VMEM((lags - 1,) + block, jnp.int16),
             pltpu.VMEM((lags - 1,) + block, jnp.int16),
             pltpu.VMEM((lags - 1, 8, 128), F32),
             pltpu.VMEM((lags - 1, 8, 128), F32),
-            pltpu.VMEM((lags,) + block, F32),
+            pltpu.VMEM((groups,) + double, F32),
             pltpu.VMEM((clusters, slots, terms), F32),
             pltpu.VMEM((8, terms), F32),
             pltpu.VMEM((lags - 1, 8, terms), F32),
@@ -268,8 +266,8 @@
             pltpu.VMEM((clusters * 8, panels), F32),
             pltpu.VMEM(block, F32),
             dma, dma((clusters,)), dma, dma,
-            dma((2, lags - 1)), dma((2, lags, 2)), dma((2, lags)), dma((2, lags - 1)),
-            dma((2, lags)), dma((2, lags - 1)),
+            dma((2, lags - 1)), dma((2, groups, 2)), dma((2, groups)), dma((2, lags - 1)),
+            dma((2, groups)), dma((2, lags - 1)),
             dma((2, clusters - 1)), dma((2, lags - 1)), dma((2, clusters - 1)),
         ],
         compiler_params=pltpu.CompilerParams(

time: 29.1 us -> 28.3 us (0.973)
  local copies, waits for them, and re-layouts: 1.38 us -> 0.62 us
    unnamed x1, local copies, waits for them, and re-layouts: 1.38 us -> 0.62 us
where the time goes in v4:
time: 28.3 us; the launch traced here: 28.1 us
  Pallas kernels  27.5 us (97%)
  local copies, waits for them, and re-layouts  0.62 us (2%)
    pallas_call x1, Pallas kernels, shards_kernel(): pl.pallas_call(functools.partial(body, lags, clusters), out_shape=pltpu.V...  27.5 us
    unnamed x1, local copies, waits for them, and re-layouts  0.62 us

profile of v4, /device:TPU:0, one launch (start us, length us, event | category | flops | bytes accessed | tf_op | source)
XLA Modules:
  0.0 28.1 jit_solution(13946747552089414255)
XLA Ops:
  0.0 27.5 %shard_map.82 = bf16[32,512]{1,0:T(8,128)(2,1)S(1)} custom-call(bf16[8,32,512]{2,1,0:T(8,128)(2,1)} %history.1, bf16[2,512,2048]{2,1,0:T(8,128)(2,1)} %kernel.1, bf16[8,256]{1,0:T(8,128)(2,1)} %bitcast.1, bf16[1,3,2,256,256]{4,3,2,1,0:T(8,128)(2,1)} %coupling.1, f32[256,2048]{1,0:T(8,128)} %evaluation.1, s32[8]{0:T(128)} %offsets.1, s32[4,3]{1,0:T(4,128)} %pair_sources.1, ...), custom_call_target="tpu_custom_call" | custom-call | flops 536870912 | bytes 4194304 | tf_op jit(solution)/shard_map/pallas_call | solution.py:239
  27.5 0.6 %copy.10 = bf16[32,512]{1,0:T(8,128)(2,1)} copy(bf16[32,512]{1,0:T(8,128)(2,1)S(1)} %shard_map.82) | data formatting | bytes 65536

commit v5 on v4

--- a/solution.py
+++ b/solution.py
@@ -46,13 +46,13 @@
 
 def body(
     lags, clusters,
-    history, kernel, moments, coupling, evaluation, offsets, pair_sources, body_cluster,
+    history, kernel, moments, coupling, evaluation, offsets_in, sources_in, cluster_in,
     out,
-    hist, weights, mats, eval_block,
+    offsets, pair_sources, body_cluster, moment_rows, hist, weights, mats, eval_block,
     rows, hist_send,
     core_send, core_recv, row_send, row_recv, row_scale, row_scaled, lag_send, lag_recv, lag_scale, lag_scaled, kept,
     moment_all, part_send, part_recv, local_all, far_rows, far,
-    hist_sem, weight_sem, mats_sem, eval_sem,
+    small_sem, hist_sem, weight_sem, mats_sem, eval_sem,
     hist_sems, core_sems, row_sems, lag_sems, row_scale_sems, lag_scale_sems, moment_sems, part_sems, local_sems,
 ):
     farm = lax.axis_index("farm")
@@ -62,9 +62,25 @@
     lags_here = kernel.shape[0]
     pairs = coupling.shape[1]
 
-    blocks = [flipped(clus, 3), flipped(clus, 2), flipped(clus, 1), clus]
+    lag_peers = [(farm, clus, flipped(lag, j)) for j in range(lags)]
+    clus_peers = [(farm, flipped(clus, r), lag) for r in range(clusters)]
+    barrier = pltpu.get_barrier_semaphore()
+    for peer in lag_peers[1:] + clus_peers[1:]:
+        pl.semaphore_signal(barrier, inc=1, device_id=peer, device_id_type=MESH)
+
+    small = [
+        pltpu.make_async_copy(src, dst, small_sem.at[i])
+        for i, (src, dst) in enumerate((
+            (offsets_in, offsets), (sources_in, pair_sources),
+            (cluster_in, body_cluster), (moments, moment_rows),
+        ))
+    ]
+    small[0].start()
     hist_in = pltpu.make_async_copy(history, hist, hist_sem)
     hist_in.start()
+    for copy in small[1:]:
+        copy.start()
+    blocks = [flipped(clus, 3), flipped(clus, 2), flipped(clus, 1), clus]
     weights_in = []
     for quad in range(clusters):
         columns = pl.ds(pl.multiple_of(blocks[quad] * panels, panels), panels)
@@ -80,18 +96,14 @@
     eval_in = pltpu.make_async_copy(evaluation.at[:, my_columns], eval_block, eval_sem)
     eval_in.start()
 
-    lag_peers = [(farm, clus, flipped(lag, j)) for j in range(lags)]
-    clus_peers = [(farm, flipped(clus, r), lag) for r in range(clusters)]
-    barrier = pltpu.get_barrier_semaphore()
-    for peer in lag_peers[1:] + clus_peers[1:]:
-        pl.semaphore_signal(barrier, inc=1, device_id=peer, device_id_type=MESH)
-
-    moment_all[clus] = moments[...].astype(F32)
+    small[0].wait()
     hist_in.wait()
     for l in range(lags_here):
         rows[l, 0:bodies] = hist[offsets[lag * lags_here + l]]
         for j in range(1, lags):
             hist_send[j - 1, l] = hist[offsets[lag_peers[j][2] * lags_here + l]]
+    small[3].wait()
+    moment_all[clus] = moment_rows[...].astype(F32)
     pl.semaphore_wait(barrier, lags - 1 + clusters - 1)
 
     sent = []
@@ -169,6 +181,7 @@
                     send(lag_scale.at[i], lag_scaled.at[i], lag_scale_sems, (i,), lag_peers[j]),
                 )
 
+    small[1].wait()
     mats_in.wait()
     for copy in moment_copies:
         copy.wait_recv()
@@ -202,6 +215,7 @@
 
     finish(0)
 
+    small[2].wait()
     eval_in.wait()
     for copy in local_copies:
         copy.wait_recv()
@@ -233,15 +247,18 @@
     dma = pltpu.SemaphoreType.DMA
     anywhere = pl.BlockSpec(memory_space=pl.ANY)
     vmem = pl.BlockSpec(memory_space=pltpu.VMEM)
-    smem = pl.BlockSpec(memory_space=pltpu.SMEM)
     block, double, groups = (bodies, panels), (2 * bodies, panels), lags // 2
     flops = 2 * lags * bodies * lags_here * depth * clusters * panels
     return pl.pallas_call(
         functools.partial(body, lags, clusters),
         out_shape=pltpu.VMEM(block, BF16),
-        in_specs=[anywhere, anywhere, vmem, anywhere, anywhere, smem, smem, smem],
+        in_specs=[anywhere] * 8,
         out_specs=vmem,
         scratch_shapes=[
+            pltpu.SMEM(offsets.shape, jnp.int32),
+            pltpu.SMEM(pair_sources.shape, jnp.int32),
+            pltpu.SMEM(body_cluster.shape, jnp.int32),
+            pltpu.VMEM((slots, terms), BF16),
             pltpu.VMEM((slots,) + block, BF16),
             pltpu.VMEM((clusters, lags_here, depth, panels), BF16),
             pltpu.VMEM((pairs, lags_here, terms, terms), BF16),
@@ -265,7 +282,7 @@
             pltpu.VMEM((clusters, 8, terms), F32),
             pltpu.VMEM((clusters * 8, panels), F32),
             pltpu.VMEM(block, F32),
-            dma, dma((clusters,)), dma, dma,
+            dma((4,)), dma, dma((clusters,)), dma, dma,
             dma((2, lags - 1)), dma((2, groups, 2)), dma((2, groups)), dma((2, lags - 1)),
             dma((2, groups)), dma((2, lags - 1)),
             dma((2, clusters - 1)), dma((2, lags - 1)), dma((2, clusters - 1)),

time: 28.3 us -> 27.4 us (0.968)
  Pallas kernels: 27.5 us -> 26.7 us
    pallas_call x1, Pallas kernels: 27.5 us -> 26.7 us  [shards_kernel(): pl.pallas_call(functools.partial(body, lags, clusters), out_shape=pltpu.V...]
where the time goes in v5:
time: 27.4 us; the launch traced here: 27.3 us
  Pallas kernels  26.7 us (97%)
  local copies, waits for them, and re-layouts  0.62 us (2%)
    pallas_call x1, Pallas kernels, shards_kernel(): pl.pallas_call(functools.partial(body, lags, clusters), out_shape=pltpu.V...  26.7 us
    unnamed x1, local copies, waits for them, and re-layouts  0.62 us

profile of v5, /device:TPU:0, one launch (start us, length us, event | category | flops | bytes accessed | tf_op | source)
XLA Modules:
  0.0 27.3 jit_solution(8139285006385514363)
XLA Ops:
  0.0 26.7 %shard_map.82 = bf16[32,512]{1,0:T(8,128)(2,1)S(1)} custom-call(bf16[8,32,512]{2,1,0:T(8,128)(2,1)} %history.1, bf16[2,512,2048]{2,1,0:T(8,128)(2,1)} %kernel.1, bf16[8,256]{1,0:T(8,128)(2,1)} %bitcast.1, bf16[1,3,2,256,256]{4,3,2,1,0:T(8,128)(2,1)} %coupling.1, f32[256,2048]{1,0:T(8,128)} %evaluation.1, s32[8]{0:T(128)} %offsets_in.1, s32[4,3]{1,0:T(4,128)} %sources_in.1, ...), custom_call_target="tpu_custom_call" | custom-call | flops 536870912 | bytes 4194304 | tf_op jit(solution)/shard_map/pallas_call | solution.py:252
  26.7 0.6 %copy.10 = bf16[32,512]{1,0:T(8,128)(2,1)} copy(bf16[32,512]{1,0:T(8,128)(2,1)S(1)} %shard_map.82) | data formatting | bytes 65536

commit v6 on v5

--- a/solution.py
+++ b/solution.py
@@ -10,6 +10,9 @@
 MESH = pl.DeviceIdType.MESH
 F32 = jnp.float32
 BF16 = jnp.bfloat16
+
+
+GROUPS = ((0,), (1, 2), (3,))
 
 
 def flipped(index, bits):
@@ -128,58 +131,70 @@
         for r in range(1, clusters)
     ]
 
-    hist_copies[3] = send_history(3)
     core_copies, row_copies, lag_copies = {}, {}, {}
 
-    height = 2 * bodies
+    def spans(group):
+        return GROUPS[group][0] * bodies, len(GROUPS[group]) * bodies
 
     def product(group, quad):
         if group == 0:
             weights_in[quad].wait()
+        top, height = spans(group)
         total = None
         for l in range(lags_here):
             term = jnp.dot(
-                rows[l, group * height : (group + 1) * height], weights[quad, l],
-                preferred_element_type=F32,
+                rows[l, top : top + height], weights[quad, l], preferred_element_type=F32
             )
             total = term if total is None else total + term
         return total
 
     def begin(group):
-        for j in (2 * group, 2 * group + 1):
+        for j in GROUPS[group]:
             if j > 0:
                 hist_copies[j].wait_recv()
+        part = pl.ds(0, spans(group)[1])
         for side, quad in ((0, 0), (1, 2)):
-            core_send[group, side] = product(group, quad)
+            core_send[group, side, part] = product(group, quad)
             core_copies[group, side] = send(
-                core_send.at[group, side], core_recv.at[group, side],
+                core_send.at[group, side, part], core_recv.at[group, side, part],
                 core_sems, (group, side), clus_peers[1],
             )
+            if group == 0 and side == 0:
+                hist_copies[3] = send_history(3)
         other = product(group, 1)
         core_copies[group, 0].wait_recv()
-        encode(other + core_recv[group, 0], row_send.at[group], row_scale.at[group])
+        encode(other + core_recv[group, 0, part], row_send.at[group, part], row_scale.at[group])
         row_copies[group] = (
-            send(row_send.at[group], row_recv.at[group], row_sems, (group,), clus_peers[2]),
-            send(row_scale.at[group], row_scaled.at[group], row_scale_sems, (group,), clus_peers[2]),
+            send(
+                row_send.at[group, part], row_recv.at[group, part],
+                row_sems, (group,), clus_peers[2],
+            ),
+            send(
+                row_scale.at[group], row_scaled.at[group],
+                row_scale_sems, (group,), clus_peers[2],
+            ),
         )
         mine = product(group, 3)
         core_copies[group, 1].wait_recv()
-        kept[group] = mine + core_recv[group, 1]
+        kept[group, part] = mine + core_recv[group, 1, part]
 
     def finish(group):
         for copy in row_copies[group]:
             copy.wait_recv()
-        total = kept[group] + decode(row_recv.at[group], row_scaled.at[group])
+        part = pl.ds(0, spans(group)[1])
+        total = kept[group, part] + decode(row_recv.at[group, part], row_scaled.at[group])
         if group == 0:
-            kept[0] = total
-        for j in (2 * group, 2 * group + 1):
+            kept[0, part] = total
+        for at, j in enumerate(GROUPS[group]):
             if j > 0:
-                i, top = j - 1, (j - 2 * group) * bodies
+                i, top = j - 1, at * bodies
                 encode(total[top : top + bodies], lag_send.at[i], lag_scale.at[i])
                 lag_copies[j] = (
                     send(lag_send.at[i], lag_recv.at[i], lag_sems, (i,), lag_peers[j]),
                     send(lag_scale.at[i], lag_scaled.at[i], lag_scale_sems, (i,), lag_peers[j]),
                 )
+
+    begin(0)
 
     small[1].wait()
     mats_in.wait()
@@ -201,7 +216,8 @@
         for j in range(1, lags)
     ]
 
-    begin(0)
+    begin(1)
+    finish(0)
 
     local = part_send[...]
     for j in range(1, lags):
@@ -213,7 +229,9 @@
         for r in range(1, clusters)
     ]
 
-    finish(0)
+    finish(1)
+    begin(2)
+    finish(2)
 
     small[2].wait()
     eval_in.wait()
@@ -226,8 +244,6 @@
     for b in range(bodies):
         far[b : b + 1, :] = far_rows[pl.ds(body_cluster[lag * bodies + b] * 8, 1), :]
 
-    begin(1)
-    finish(1)
     total = kept[0, 0:bodies]
     for j in range(1, lags):
         for copy in lag_copies[j]:
@@ -247,7 +263,7 @@
     dma = pltpu.SemaphoreType.DMA
     anywhere = pl.BlockSpec(memory_space=pl.ANY)
     vmem = pl.BlockSpec(memory_space=pltpu.VMEM)
-    block, double, groups = (bodies, panels), (2 * bodies, panels), lags // 2
+    block, double, groups = (bodies, panels), (2 * bodies, panels), len(GROUPS)
     flops = 2 * lags * bodies * lags_here * depth * clusters * panels
     return pl.pallas_call(
         functools.partial(body, lags, clusters),

time: 27.4 us -> 25.7 us (0.938)
  Pallas kernels: 26.7 us -> 25 us
    pallas_call x1, Pallas kernels: 26.7 us -> 25 us  [shards_kernel(): pl.pallas_call(functools.partial(body, lags, clusters), out_shape=pltpu.V...]
where the time goes in v6:
time: 25.7 us; the launch traced here: 25.6 us
  Pallas kernels  25 us (97%)
  local copies, waits for them, and re-layouts  0.62 us (2%)
    pallas_call x1, Pallas kernels, shards_kernel(): pl.pallas_call(functools.partial(body, lags, clusters), out_shape=pltpu.V...  25 us
    unnamed x1, local copies, waits for them, and re-layouts  0.62 us

profile of v6, /device:TPU:0, one launch (start us, length us, event | category | flops | bytes accessed | tf_op | source)
XLA Modules:
  0.0 25.6 jit_solution(8720388625755099261)
XLA Ops:
  0.0 25.0 %shard_map.82 = bf16[32,512]{1,0:T(8,128)(2,1)S(1)} custom-call(bf16[8,32,512]{2,1,0:T(8,128)(2,1)} %history.1, bf16[2,512,2048]{2,1,0:T(8,128)(2,1)} %kernel.1, bf16[8,256]{1,0:T(8,128)(2,1)} %bitcast.1, bf16[1,3,2,256,256]{4,3,2,1,0:T(8,128)(2,1)} %coupling.1, f32[256,2048]{1,0:T(8,128)} %evaluation.1, s32[8]{0:T(128)} %offsets_in.1, s32[4,3]{1,0:T(4,128)} %sources_in.1, ...), custom_call_target="tpu_custom_call" | custom-call | flops 536870912 | bytes 4194304 | tf_op jit(solution)/shard_map/pallas_call | solution.py:268
  25.0 0.6 %copy.10 = bf16[32,512]{1,0:T(8,128)(2,1)} copy(bf16[32,512]{1,0:T(8,128)(2,1)S(1)} %shard_map.82) | data formatting | bytes 65536

commit v7 on v6

--- a/solution.py
+++ b/solution.py
@@ -131,7 +131,7 @@
         for r in range(1, clusters)
     ]
 
-    core_copies, row_copies, lag_copies = {}, {}, {}
+    group_copies, lag_copies = [[] for _ in GROUPS], {}
 
     def spans(group):
         return GROUPS[group][0] * bodies, len(GROUPS[group]) * bodies
@@ -153,36 +153,37 @@
             if j > 0:
                 hist_copies[j].wait_recv()
         part = pl.ds(0, spans(group)[1])
-        for side, quad in ((0, 0), (1, 2)):
-            core_send[group, side, part] = product(group, quad)
-            core_copies[group, side] = send(
-                core_send.at[group, side, part], core_recv.at[group, side, part],
-                core_sems, (group, side), clus_peers[1],
-            )
-            if group == 0 and side == 0:
+        for quad in range(clusters - 1):
+            value, r = product(group, quad), clusters - 1 - quad
+            if r == 1:
+                core_send[group, part] = value
+                group_copies[group].append(
+                    send(
+                        core_send.at[group, part], core_recv.at[group, part],
+                        core_sems, (group,), clus_peers[1],
+                    )
+                )
+            else:
+                at = (group, r - 2)
+                encode(value, row_send.at[at + (part,)], row_scale.at[at])
+                group_copies[group] += [
+                    send(
+                        row_send.at[at + (part,)], row_recv.at[at + (part,)],
+                        row_sems, at, clus_peers[r],
+                    ),
+                    send(row_scale.at[at], row_scaled.at[at], row_scale_sems, at, clus_peers[r]),
+                ]
+            if group == 0 and quad == 0:
                 hist_copies[3] = send_history(3)
-        other = product(group, 1)
-        core_copies[group, 0].wait_recv()
-        encode(other + core_recv[group, 0, part], row_send.at[group, part], row_scale.at[group])
-        row_copies[group] = (
-            send(
-                row_send.at[group, part], row_recv.at[group, part],
-                row_sems, (group,), clus_peers[2],
-            ),
-            send(
-                row_scale.at[group], row_scaled.at[group],
-                row_scale_sems, (group,), clus_peers[2],
-            ),
-        )
-        mine = product(group, 3)
-        core_copies[group, 1].wait_recv()
-        kept[group, part] = mine + core_recv[group, 1, part]
+        kept[group, part] = product(group, clusters - 1)
 
     def finish(group):
-        for copy in row_copies[group]:
+        for copy in group_copies[group]:
             copy.wait_recv()
         part = pl.ds(0, spans(group)[1])
-        total = kept[group, part] + decode(row_recv.at[group, part], row_scaled.at[group])
+        total = kept[group, part] + core_recv[group, part]
+        for i in range(2):
+            total = total + decode(row_recv.at[group, i, part], row_scaled.at[group, i])
         if group == 0:
             kept[0, part] = total
         for at, j in enumerate(GROUPS[group]):
@@ -281,12 +282,12 @@
             pltpu.VMEM((terms, panels), F32),
             pltpu.VMEM((lags_here, lags * bodies, panels), BF16),
             pltpu.VMEM((lags - 1, lags_here) + block, BF16),
-            pltpu.VMEM((groups, 2) + double, F32),
-            pltpu.VMEM((groups, 2) + double, F32),
-            pltpu.VMEM((groups,) + double, jnp.int16),
-            pltpu.VMEM((groups,) + double, jnp.int16),
-            pltpu.VMEM((groups, 8, 128), F32),
-            pltpu.VMEM((groups, 8, 128), F32),
+            pltpu.VMEM((groups,) + double, F32),
+            pltpu.VMEM((groups,) + double, F32),
+            pltpu.VMEM((groups, 2) + double, jnp.int16),
+            pltpu.VMEM((groups, 2) + double, jnp.int16),
+            pltpu.VMEM((groups, 2, 8, 128), F32),
+            pltpu.VMEM((groups, 2, 8, 128), F32),
             pltpu.VMEM((lags - 1,) + block, jnp.int16),
             pltpu.VMEM((lags - 1,) + block, jnp.int16),
             pltpu.VMEM((lags - 1, 8, 128), F32),
@@ -299,8 +300,8 @@
             pltpu.VMEM((clusters * 8, panels), F32),
             pltpu.VMEM(block, F32),
             dma((4,)), dma, dma((clusters,)), dma, dma,
-            dma((2, lags - 1)), dma((2, groups, 2)), dma((2, groups)), dma((2, lags - 1)),
-            dma((2, groups)), dma((2, lags - 1)),
+            dma((2, lags - 1)), dma((2, groups)), dma((2, groups, 2)), dma((2, lags - 1)),
+            dma((2, groups, 2)), dma((2, lags - 1)),
             dma((2, clusters - 1)), dma((2, lags - 1)), dma((2, clusters - 1)),
         ],
         compiler_params=pltpu.CompilerParams(

time: 25.7 us -> 24.6 us (0.957)
  Pallas kernels: 25 us -> 23.8 us
    pallas_call x1, Pallas kernels: 25 us -> 23.8 us  [shards_kernel(): pl.pallas_call(functools.partial(body, lags, clusters), out_shape=pltpu.V...]
where the time goes in v7:
time: 24.6 us; the launch traced here: 24.4 us
  Pallas kernels  23.8 us (97%)
  local copies, waits for them, and re-layouts  0.62 us (3%)
    pallas_call x1, Pallas kernels, shards_kernel(): pl.pallas_call(functools.partial(body, lags, clusters), out_shape=pltpu.V...  23.8 us
    unnamed x1, local copies, waits for them, and re-layouts  0.62 us

profile of v7, /device:TPU:0, one launch (start us, length us, event | category | flops | bytes accessed | tf_op | source)
XLA Modules:
  0.0 24.4 jit_solution(3015796816036470280)
XLA Ops:
  0.0 23.8 %shard_map.82 = bf16[32,512]{1,0:T(8,128)(2,1)S(1)} custom-call(bf16[8,32,512]{2,1,0:T(8,128)(2,1)} %history.1, bf16[2,512,2048]{2,1,0:T(8,128)(2,1)} %kernel.1, bf16[8,256]{1,0:T(8,128)(2,1)} %bitcast.1, bf16[1,3,2,256,256]{4,3,2,1,0:T(8,128)(2,1)} %coupling.1, f32[256,2048]{1,0:T(8,128)} %evaluation.1, s32[8]{0:T(128)} %offsets_in.1, s32[4,3]{1,0:T(4,128)} %sources_in.1, ...), custom_call_target="tpu_custom_call" | custom-call | flops 536870912 | bytes 4194304 | tf_op jit(solution)/shard_map/pallas_call | solution.py:269
  23.8 0.6 %copy.10 = bf16[32,512]{1,0:T(8,128)(2,1)} copy(bf16[32,512]{1,0:T(8,128)(2,1)S(1)} %shard_map.82) | data formatting | bytes 65536

commit v8 on v7

--- a/solution.py
+++ b/solution.py
@@ -13,6 +13,7 @@
 
 
 GROUPS = ((0,), (1, 2), (3,))
+LAG_ORDER = (0, 1, 3, 2)
 
 
 def flipped(index, bits):
@@ -65,7 +66,7 @@
     lags_here = kernel.shape[0]
     pairs = coupling.shape[1]
 
-    lag_peers = [(farm, clus, flipped(lag, j)) for j in range(lags)]
+    lag_peers = [(farm, clus, flipped(lag, bits)) for bits in LAG_ORDER]
     clus_peers = [(farm, flipped(clus, r), lag) for r in range(clusters)]
     barrier = pltpu.get_barrier_semaphore()
     for peer in lag_peers[1:] + clus_peers[1:]:
@@ -230,8 +231,8 @@
         for r in range(1, clusters)
     ]
 
+    begin(2)
     finish(1)
-    begin(2)
     finish(2)
 
     small[2].wait()

time: 24.6 us -> 22.8 us (0.927)
  Pallas kernels: 23.8 us -> 22 us
    pallas_call x1, Pallas kernels: 23.8 us -> 22 us  [shards_kernel(): pl.pallas_call(functools.partial(body, lags, clusters), out_shape=pltpu.V...]
where the time goes in v8:
time: 22.8 us; the launch traced here: 22.6 us
  Pallas kernels  22 us (96%)
  local copies, waits for them, and re-layouts  0.62 us (3%)
    pallas_call x1, Pallas kernels, shards_kernel(): pl.pallas_call(functools.partial(body, lags, clusters), out_shape=pltpu.V...  22 us
    unnamed x1, local copies, waits for them, and re-layouts  0.62 us

profile of v8, /device:TPU:0, one launch (start us, length us, event | category | flops | bytes accessed | tf_op | source)
XLA Modules:
  0.0 22.6 jit_solution(8296367267832272130)
XLA Ops:
  0.0 22.0 %shard_map.82 = bf16[32,512]{1,0:T(8,128)(2,1)S(1)} custom-call(bf16[8,32,512]{2,1,0:T(8,128)(2,1)} %history.1, bf16[2,512,2048]{2,1,0:T(8,128)(2,1)} %kernel.1, bf16[8,256]{1,0:T(8,128)(2,1)} %bitcast.1, bf16[1,3,2,256,256]{4,3,2,1,0:T(8,128)(2,1)} %coupling.1, f32[256,2048]{1,0:T(8,128)} %evaluation.1, s32[8]{0:T(128)} %offsets_in.1, s32[4,3]{1,0:T(4,128)} %sources_in.1, ...), custom_call_target="tpu_custom_call" | custom-call | flops 536870912 | bytes 4194304 | tf_op jit(solution)/shard_map/pallas_call | solution.py:270
  22.0 0.6 %copy.10 = bf16[32,512]{1,0:T(8,128)(2,1)} copy(bf16[32,512]{1,0:T(8,128)(2,1)S(1)} %shard_map.82) | data formatting | bytes 65536

commit v9 on v8

--- a/solution.py
+++ b/solution.py
@@ -54,7 +54,7 @@
     out,
     offsets, pair_sources, body_cluster, moment_rows, hist, weights, mats, eval_block,
     rows, hist_send,
-    core_send, core_recv, row_send, row_recv, row_scale, row_scaled, lag_send, lag_recv, lag_scale, lag_scaled, kept,
+    core_send, core_recv, row_send, row_recv, row_scale, row_scaled, lag_send, lag_recv, lag_scale, lag_scaled, kept, early,
     moment_all, part_send, part_recv, local_all, far_rows, far,
     small_sem, hist_sem, weight_sem, mats_sem, eval_sem,
     hist_sems, core_sems, row_sems, lag_sems, row_scale_sems, lag_scale_sems, moment_sems, part_sems, local_sems,
@@ -123,8 +123,13 @@
         return copy
 
     def send_history(j):
-        landing = rows.at[:, pl.ds(j * bodies, bodies)]
-        return send(hist_send.at[j - 1], landing, hist_sems, (j - 1,), lag_peers[j])
+        return [
+            send(
+                hist_send.at[j - 1, l], rows.at[l, pl.ds(j * bodies, bodies)],
+                hist_sems, (j - 1, l), lag_peers[j],
+            )
+            for l in range(lags_here)
+        ]
 
     hist_copies = {j: send_history(j) for j in (2, 1)}
     moment_copies = [
@@ -134,6 +139,8 @@
 
     group_copies, lag_copies = [[] for _ in GROUPS], {}
 
+    last = len(GROUPS) - 1
+
     def spans(group):
         return GROUPS[group][0] * bodies, len(GROUPS[group]) * bodies
 
@@ -141,8 +148,8 @@
         if group == 0:
             weights_in[quad].wait()
         top, height = spans(group)
-        total = None
-        for l in range(lags_here):
+        total = early[quad] if group == last else None
+        for l in range(lags_here - 1 if group == last else 0, lags_here):
             term = jnp.dot(
                 rows[l, top : top + height], weights[quad, l], preferred_element_type=F32
             )
@@ -150,9 +157,17 @@
         return total
 
     def begin(group):
-        for j in GROUPS[group]:
-            if j > 0:
-                hist_copies[j].wait_recv()
+        arriving = [hist_copies[j] for j in GROUPS[group] if j > 0]
+        for l in range(lags_here):
+            for copies in arriving:
+                copies[l].wait_recv()
+            if group == last and l < lags_here - 1:
+                top, height = spans(group)
+                for quad in range(clusters):
+                    term = jnp.dot(
+                        rows[l, top : top + height], weights[quad, l], preferred_element_type=F32
+                    )
+                    early[quad] = term if l == 0 else early[quad] + term
         part = pl.ds(0, spans(group)[1])
         for quad in range(clusters - 1):
             value, r = product(group, quad), clusters - 1 - quad
@@ -294,6 +309,7 @@
             pltpu.VMEM((lags - 1, 8, 128), F32),
             pltpu.VMEM((lags - 1, 8, 128), F32),
             pltpu.VMEM((groups,) + double, F32),
+            pltpu.VMEM((clusters,) + block, F32),
             pltpu.VMEM((clusters, slots, terms), F32),
             pltpu.VMEM((8, terms), F32),
             pltpu.VMEM((lags - 1, 8, terms), F32),
@@ -301,7 +317,7 @@
             pltpu.VMEM((clusters * 8, panels), F32),
             pltpu.VMEM(block, F32),
             dma((4,)), dma, dma((clusters,)), dma, dma,
-            dma((2, lags - 1)), dma((2, groups)), dma((2, groups, 2)), dma((2, lags - 1)),
+            dma((2, lags - 1, lags_here)), dma((2, groups)), dma((2, groups, 2)), dma((2, lags - 1)),
             dma((2, groups, 2)), dma((2, lags - 1)),
             dma((2, clusters - 1)), dma((2, lags - 1)), dma((2, clusters - 1)),
         ],

time: 22.8 us -> 22.9 us (level)
  no operation moved by 1% of the time
where the time goes in v9:
time: 22.9 us; the launch traced here: 22.8 us
  Pallas kernels  22.2 us (97%)
  local copies, waits for them, and re-layouts  0.62 us (3%)
    pallas_call x1, Pallas kernels, shards_kernel(): pl.pallas_call(functools.partial(body, lags, clusters), out_shape=pltpu.V...  22.2 us
    unnamed x1, local copies, waits for them, and re-layouts  0.62 us

profile of v9, /device:TPU:0, one launch (start us, length us, event | category | flops | bytes accessed | tf_op | source)
XLA Modules:
  0.0 22.8 jit_solution(12355286417462490200)
XLA Ops:
  0.0 22.2 %shard_map.82 = bf16[32,512]{1,0:T(8,128)(2,1)S(1)} custom-call(bf16[8,32,512]{2,1,0:T(8,128)(2,1)} %history.1, bf16[2,512,2048]{2,1,0:T(8,128)(2,1)} %kernel.1, bf16[8,256]{1,0:T(8,128)(2,1)} %bitcast.1, bf16[1,3,2,256,256]{4,3,2,1,0:T(8,128)(2,1)} %coupling.1, f32[256,2048]{1,0:T(8,128)} %evaluation.1, s32[8]{0:T(128)} %offsets_in.1, s32[4,3]{1,0:T(4,128)} %sources_in.1, ...), custom_call_target="tpu_custom_call" | custom-call | flops 536870912 | bytes 4194304 | tf_op jit(solution)/shard_map/pallas_call | solution.py:285
  22.2 0.6 %copy.10 = bf16[32,512]{1,0:T(8,128)(2,1)} copy(bf16[32,512]{1,0:T(8,128)(2,1)S(1)} %shard_map.82) | data formatting | bytes 65536

commit v10 on v8

--- a/solution.py
+++ b/solution.py
@@ -126,7 +126,7 @@
         landing = rows.at[:, pl.ds(j * bodies, bodies)]
         return send(hist_send.at[j - 1], landing, hist_sems, (j - 1,), lag_peers[j])
 
-    hist_copies = {j: send_history(j) for j in (2, 1)}
+    hist_copies = {j: send_history(j) for j in (2, 1, 3)}
     moment_copies = [
         send(moment_all.at[clus], moment_all.at[clus], moment_sems, (r - 1,), clus_peers[r])
         for r in range(1, clusters)
@@ -174,8 +174,6 @@
                     ),
                     send(row_scale.at[at], row_scaled.at[at], row_scale_sems, at, clus_peers[r]),
                 ]
-            if group == 0 and quad == 0:
-                hist_copies[3] = send_history(3)
         kept[group, part] = product(group, clusters - 1)
 
     def finish(group):

time: 22.8 us -> 22.8 us (level)
  no operation moved by 1% of the time
where the time goes in v10:
time: 22.8 us; the launch traced here: 22.6 us
  Pallas kernels  22 us (96%)
  local copies, waits for them, and re-layouts  0.62 us (3%)
    pallas_call x1, Pallas kernels, shards_kernel(): pl.pallas_call(functools.partial(body, lags, clusters), out_shape=pltpu.V...  22 us
    unnamed x1, local copies, waits for them, and re-layouts  0.62 us

profile of v10, /device:TPU:0, one launch (start us, length us, event | category | flops | bytes accessed | tf_op | source)
XLA Modules:
  0.0 22.6 jit_solution(10482881448124554732)
XLA Ops:
  0.0 22.0 %shard_map.82 = bf16[32,512]{1,0:T(8,128)(2,1)S(1)} custom-call(bf16[8,32,512]{2,1,0:T(8,128)(2,1)} %history.1, bf16[2,512,2048]{2,1,0:T(8,128)(2,1)} %kernel.1, bf16[8,256]{1,0:T(8,128)(2,1)} %bitcast.1, bf16[1,3,2,256,256]{4,3,2,1,0:T(8,128)(2,1)} %coupling.1, f32[256,2048]{1,0:T(8,128)} %evaluation.1, s32[8]{0:T(128)} %offsets_in.1, s32[4,3]{1,0:T(4,128)} %sources_in.1, ...), custom_call_target="tpu_custom_call" | custom-call | flops 536870912 | bytes 4194304 | tf_op jit(solution)/shard_map/pallas_call | solution.py:268
  22.0 0.6 %copy.10 = bf16[32,512]{1,0:T(8,128)(2,1)} copy(bf16[32,512]{1,0:T(8,128)(2,1)S(1)} %shard_map.82) | data formatting | bytes 65536
